TPU v7x, 32 devices: a whole 2x2x4 slice. The times are simulated.
32 devices in a mesh: pipe: 2 (over core), seq: 16 (over z, y, x).
Axes of the slice: x: 2, y: 2, z: 4, core: 2. Of those that a mesh axis runs over, the one named last changes fastest.
Arguments:
- queries: bfloat16 [2, 1024, 4096], P('pipe', 'seq'), may hold values from -6 to 6
- keys: bfloat16 [2, 1024, 4096], P('pipe', 'seq'), may hold values from -6 to 6
- values: bfloat16 [2, 1024, 4096], P('pipe', 'seq'), may hold values from -6 to 6
- out_weight: bfloat16 [2, 4096, 5120], P('pipe', None, 'seq'), may hold values from -0.375 to 0.375
- head_class: int32 [2, 32], P('pipe'), may hold values from 0 to 1
- kv_blocks: int32 [2, 32, 16, 16], P('pipe'), may hold values from 0 to 15, as said below
- kv_count: int32 [2, 32], P('pipe'), may hold values from 1 to 16, as said below
Outputs:
- handed: bfloat16 [2, 1024, 5120], P('pipe', 'seq')
Inputs may be any that keep to these rules, and one draw needn't show every extreme that they name: `kv_blocks`: in every row the entries are distinct, and the first is the query block itself. `kv_count`: in every section some head uses all 16 entries.
All inputs are finite; a program needn't handle non-finite values.
Results may differ from a plain program's by a relative error of at most 0.018.
Values may be sent and summed in bfloat16 or wider, within the bound.
A program may use at most 64 MiB of HBM per device.

v0:
```python
import functools

import jax
import jax.numpy as jnp
from jax import lax
from jax.experimental import pallas as pl
from jax.experimental.pallas import tpu as pltpu
from jax.sharding import PartitionSpec as P

FRAMES = 4
BLOCK = 64
MASKED = 131072.0
LOG2E = 1.4426950408889634
TILE = 256
AHEAD = 3
MESH = pl.DeviceIdType.MESH


def kernel(
    members, per_dev, stages,
    classes, counts, lists, queries, keys, values, weight,
    out,
    qbuf, kbuf, vbuf, ebuf, bbuf, abuf, wboth, cown, csend, crecv, osend, obuf,
    qkv_send, qkv_recv, qkv_local, w_sems, w_local, up_send, down_send, side_send, a_recv,
    c_send, c_recv, o_send, o_recv,
):
    stage = lax.axis_index("pipe")
    me = lax.axis_index("seq")
    half = lax.rem(me, 2)
    col = me // 2
    side = lax.rem(col, 2)
    level = col // 2
    levels = members // 4
    cols = members // 2
    partner = me + 1 - 2 * half
    across = me + 2 - 4 * side
    following = lax.rem(stage + 1, stages)
    preceding = lax.rem(stage + stages - 1, stages)
    rows, width = queries.shape[0], kbuf.shape[-1]
    tokens = rows * members
    depth = per_dev * width
    out_cols = weight.shape[0]
    tile = TILE
    chunks = tokens // tile
    group = tile // rows
    tensors = ((queries, qbuf), (keys, kbuf), (values, vbuf))

    def block_at(chunk, place):
        return place * chunks + lax.rem(chunk + place, chunks)

    barrier = pltpu.get_barrier_semaphore()

    def greet(r, carry):
        pl.semaphore_signal(
            barrier, inc=1, device_id={"seq": lax.rem(me + r, members)}, device_id_type=MESH
        )
        return carry

    def greet_preceding(r, carry):
        pl.semaphore_signal(barrier, inc=1, device_id=(preceding, r), device_id_type=MESH)
        return carry

    lax.fori_loop(1, members, greet, 0)
    lax.fori_loop(0, members, greet_preceding, 0)

    def head_columns(owner, slot):
        return pl.ds(pl.multiple_of((owner * per_dev + slot) * width, width), width)

    my_place = me // chunks
    my_chunk = lax.rem(lax.rem(me, chunks) + chunks * group - my_place, chunks)
    mine = pl.ds(pl.multiple_of((my_chunk * group + my_place) * rows, rows), rows)
    own_copies = []
    for slot in range(per_dev):
        for which, (source, landing) in enumerate(tensors):
            copy = pltpu.make_async_copy(
                source.at[:, head_columns(me, slot)],
                landing.at[slot, mine],
                qkv_local.at[slot, which],
            )
            copy.start()
            own_copies.append(copy)
    pl.semaphore_wait(barrier, 2 * members - 1)

    for slot in range(per_dev):

        def send(r, carry):
            peer = lax.rem(me + r * (members // 2 - 1), members)
            for which, (source, landing) in enumerate(tensors):
                pltpu.make_async_remote_copy(
                    src_ref=source.at[:, head_columns(peer, slot)],
                    dst_ref=landing.at[slot, mine],
                    send_sem=qkv_send.at[slot, which],
                    recv_sem=qkv_recv.at[slot, which],
                    device_id={"seq": peer},
                    device_id_type=MESH,
                ).start()
            return carry

        lax.fori_loop(1, members, send, 0)

    def weight_columns(column, which_half):
        return pl.ds(pl.multiple_of((2 * column + which_half) * depth, depth), depth)

    def own_weight(column, carry):
        pltpu.make_async_copy(
            weight.at[:, weight_columns(column, half)],
            wboth.at[pl.ds(0, out_cols), pl.ds(pl.multiple_of(column * depth, depth), depth)],
            w_local,
        ).start()
        return carry

    lax.fori_loop(0, cols, own_weight, 0)

    nblock = lists.shape[0]
    place = lax.broadcasted_iota(jnp.int32, (tokens, width), 0)
    lane = lax.broadcasted_iota(jnp.int32, (tokens, width), 1)
    token = block_at(place // tile, lax.rem(place, tile) // rows) * rows + lax.rem(place, rows)
    spatial = token // BLOCK
    temporal = lax.rem(token, tokens // FRAMES) // (BLOCK // FRAMES)
    every = lists[...].astype(jnp.float32)
    head_lane = lax.broadcasted_iota(jnp.int32, every.shape, 2)
    entry = lax.broadcasted_iota(jnp.int32, every.shape[:2] + (width,), 1)
    listed_lane = lax.broadcasted_iota(jnp.int32, entry.shape, 2).astype(jnp.float32)
    for slot in range(per_dev):
        head = me * per_dev + slot
        block_of = jnp.where(classes[0, head] == 1, temporal, spatial)
        member = jnp.where(block_of == lane, 1.0, 0.0).astype(jnp.bfloat16)
        ebuf[slot] = member
        entries = jnp.sum(jnp.where(head_lane == head, every, 0.0), axis=2, keepdims=True)
        usable = jnp.where(entry < counts[0, head], 0.0, -MASKED)
        offset = jnp.max(jnp.where(entries == listed_lane, usable, -MASKED), axis=1)
        offset = jnp.concatenate(
            [offset, jnp.zeros((width - nblock, width), jnp.float32)], axis=0
        ).astype(jnp.bfloat16)
        bbuf[slot] = lax.dot_general(
            member, offset, (((1,), (1,)), ((), ())), preferred_element_type=jnp.float32
        ).astype(jnp.bfloat16)
    for copy in own_copies:
        copy.wait()

    scale = LOG2E * width ** (-0.5)
    others = pl.ds(0, tokens - rows)

    def chunk_rows(chunk):
        return pl.ds(pl.multiple_of(chunk * tile, tile), tile)

    def piece_copy(source_level, slot, chunk, target, sems):
        column = 2 * source_level + side
        piece = abuf.at[column, slot, chunk_rows(chunk)]
        return pltpu.make_async_remote_copy(
            src_ref=piece,
            dst_ref=piece,
            send_sem=sems.at[slot, chunk, source_level],
            recv_sem=a_recv.at[column, slot, chunk],
            device_id={"seq": target},
            device_id_type=MESH,
        )

    def received(column, slot, chunk):
        piece = abuf.at[column, slot, chunk_rows(chunk)]
        pltpu.make_async_copy(piece, piece, a_recv.at[column, slot, chunk]).wait()

    def send_up(source_level, slot, chunk):
        @pl.when(level + 1 < levels)
        def _():
            piece_copy(source_level, slot, chunk, me + 4, up_send).start()

    def send_down(source_level, slot, chunk):
        @pl.when(level >= 1)
        def _():
            piece_copy(source_level, slot, chunk, me - 4, down_send).start()

    def send_side(source_level, slot, chunk):
        piece_copy(source_level, slot, chunk, across, side_send).start()

    def attend(slot, then):
        for which, (source, landing) in enumerate(tensors):
            span = landing.at[slot, others]
            pltpu.make_async_copy(span, span, qkv_recv.at[slot, which]).wait()

        def step(chunk, carry):
            here = chunk_rows(chunk)
            wide_query = jnp.concatenate([qbuf[slot, here], ebuf[slot, here]], axis=1)
            wide_key = jnp.concatenate([kbuf[slot], bbuf[slot]], axis=1)
            scores = lax.dot_general(
                wide_query, wide_key, (((1,), (1,)), ((), ())), preferred_element_type=jnp.float32
            )
            top = jnp.max(scores, axis=1, keepdims=True)
            probs = jnp.exp2((scores - top) * scale).astype(jnp.bfloat16)
            wide_value = jnp.concatenate(
                [vbuf[slot], jnp.ones((tokens, width), jnp.bfloat16)], axis=1
            )
            sums = jnp.dot(probs, wide_value, preferred_element_type=jnp.float32)
            abuf[col, slot, here] = (sums[:, :width] / sums[:, width:]).astype(jnp.bfloat16)
            send_up(level, slot, chunk)
            send_down(level, slot, chunk)
            send_side(level, slot, chunk)
            if then is not None:
                then(chunk)
            return carry

        lax.fori_loop(0, chunks, step, 0)

    def relay(slot, chunk, first, last):
        def hop(t, carry):
            below = level - 1 - t
            above = level + 1 + t

            @pl.when(below >= 0)
            def _():
                received(2 * below + side, slot, chunk)
                send_up(below, slot, chunk)
                send_side(below, slot, chunk)

            @pl.when(above < levels)
            def _():
                received(2 * above + side, slot, chunk)
                send_down(above, slot, chunk)
                send_side(above, slot, chunk)

            return carry

        lax.fori_loop(first, last, hop, 0)

    def relay_all(slot, first, last):
        def step(chunk, carry):
            relay(slot, chunk, first, last)
            return carry

        lax.fori_loop(0, chunks, step, 0)

    weight_span = wboth.at[pl.ds(out_cols, out_cols)]
    for slot in range(per_dev):
        before = None
        if slot > 0:
            before = functools.partial(relay, slot - 1, first=1, last=2)
        attend(slot, before)
        if slot == 0:

            def swap_weight(column, carry):
                pltpu.make_async_remote_copy(
                    src_ref=weight.at[:, weight_columns(column, 1 - half)],
                    dst_ref=wboth.at[
                        pl.ds(out_cols, out_cols),
                        pl.ds(pl.multiple_of(column * depth, depth), depth),
                    ],
                    send_sem=w_sems.at[0],
                    recv_sem=w_sems.at[1],
                    device_id={"seq": partner},
                    device_id_type=MESH,
                ).start()
                return carry

            lax.fori_loop(0, cols, swap_weight, 0)
        else:
            relay_all(slot - 1, 2, levels - 1)
        if slot < per_dev - 1:
            relay_all(slot, 0, 1)

    def relay_last(chunk, carry):
        relay(per_dev - 1, chunk, 0, levels - 1)
        return carry

    lax.fori_loop(0, AHEAD, relay_last, 0)
    weight_own = wboth.at[pl.ds(0, out_cols)]
    pltpu.make_async_copy(weight_own, weight_own, w_local).wait()
    pltpu.make_async_copy(weight_span, weight_span, w_sems.at[1]).wait()

    def chunk_copy(chunk):
        here = chunk_rows(chunk)
        return pltpu.make_async_remote_copy(
            src_ref=csend.at[here],
            dst_ref=crecv.at[here],
            send_sem=c_send.at[chunk],
            recv_sem=c_recv.at[chunk],
            device_id={"seq": partner},
            device_id_type=MESH,
        )

    def row_copy(chunk, q):
        start = pl.multiple_of((chunk * group + q) * rows, rows)
        return pltpu.make_async_remote_copy(
            src_ref=osend.at[pl.ds(start, rows)],
            dst_ref=obuf.at[me],
            send_sem=o_send.at[chunk * group + q],
            recv_sem=o_recv.at[me],
            device_id=(following, block_at(chunk, q)),
            device_id_type=MESH,
        )

    def hand(chunk):
        here = chunk_rows(chunk)
        chunk_copy(chunk).wait_recv()
        osend[here] = (cown[here] + crecv[here].astype(jnp.float32)).astype(jnp.bfloat16)
        for q in range(group):
            row_copy(chunk, lax.rem(level + q, group)).start()

    def finish(chunk, carry):
        here = chunk_rows(chunk)

        @pl.when(chunk + AHEAD < chunks)
        def _():
            relay_last(chunk + AHEAD, 0)

        def from_side(source_level, inner):
            for slot in range(per_dev):
                received(2 * source_level + 1 - side, slot, chunk)
            return inner

        lax.fori_loop(0, levels, from_side, 0)
        piece = jnp.concatenate(
            [abuf[column, slot, here] for column in range(cols) for slot in range(per_dev)], axis=1
        )
        shares = lax.dot_general(
            piece, wboth[...], (((1,), (1,)), ((), ())), preferred_element_type=jnp.float32
        )
        csend[here] = shares[:, out_cols:].astype(jnp.bfloat16)
        chunk_copy(chunk).start()
        cown[here] = shares[:, :out_cols]

        @pl.when(chunk >= 1)
        def _():
            hand(chunk - 1)

        return carry

    lax.fori_loop(0, chunks, finish, 0)
    hand(chunks - 1)

    for slot in range(per_dev):
        for which, (source, landing) in enumerate(tensors):
            span = landing.at[slot, others]
            pltpu.make_async_copy(span, span, qkv_send.at[slot, which]).wait()
    pltpu.make_async_copy(weight_span, weight_span, w_sems.at[0]).wait()

    def left(chunk, carry):
        for slot in range(per_dev):

            def from_level(source_level, inner):
                @pl.when((level + 1 < levels) & (source_level <= level))
                def _():
                    piece_copy(source_level, slot, chunk, across, up_send).wait_send()

                @pl.when((level >= 1) & (source_level >= level))
                def _():
                    piece_copy(source_level, slot, chunk, across, down_send).wait_send()

                piece_copy(source_level, slot, chunk, across, side_send).wait_send()
                return inner

            lax.fori_loop(0, levels, from_level, 0)
        chunk_copy(chunk).wait_send()
        for q in range(group):
            row_copy(chunk, q).wait_send()
        return carry

    lax.fori_loop(0, chunks, left, 0)

    def arrived(source, carry):
        pltpu.make_async_copy(obuf.at[source], obuf.at[source], o_recv.at[source]).wait()
        return carry

    lax.fori_loop(0, members, arrived, 0)
    pair = 2 * out_cols
    for i in range(members // 2):
        out[:, i * pair : (i + 1) * pair] = jnp.concatenate([obuf[2 * i], obuf[2 * i + 1]], axis=1)


def shards(stages, queries, keys, values, out_weight, head_class, kv_blocks, kv_count):
    members = lax.axis_size("seq")
    heads = head_class.shape[1]
    per_dev = heads // members
    rows, total = queries.shape[1:]
    width = total // heads
    tokens = rows * members
    out_cols = out_weight.shape[2]
    cols = members // 2
    depth = per_dev * width
    weight = out_weight[0].T
    bf16, f32 = jnp.bfloat16, jnp.float32
    dma = pltpu.SemaphoreType.DMA
    vmem = pl.BlockSpec(memory_space=pltpu.VMEM)
    smem = pl.BlockSpec(memory_space=pltpu.SMEM)
    hbm = pl.BlockSpec(memory_space=pl.ANY)
    head_buffer = pltpu.VMEM((per_dev, tokens, width), bf16)
    levels = members // 4
    chunks = tokens // TILE
    result = pl.pallas_call(
        functools.partial(kernel, members, per_dev, stages),
        out_shape=jax.ShapeDtypeStruct((rows, members * out_cols), bf16),
        in_specs=[smem, smem, vmem, hbm, hbm, hbm, hbm],
        out_specs=vmem,
        scratch_shapes=[
            head_buffer, head_buffer, head_buffer, head_buffer, head_buffer,
            pltpu.VMEM((cols, per_dev, tokens, width), bf16),
            pltpu.VMEM((2 * out_cols, cols * depth), bf16),
            pltpu.VMEM((tokens, out_cols), f32),
            pltpu.VMEM((tokens, out_cols), bf16),
            pltpu.VMEM((tokens, out_cols), bf16),
            pltpu.VMEM((tokens, out_cols), bf16),
            pltpu.VMEM((members, rows, out_cols), bf16),
            dma((per_dev, 3)), dma((per_dev, 3)), dma((per_dev, 3)),
            dma((2,)), dma,
            dma((per_dev, chunks, levels)), dma((per_dev, chunks, levels)),
            dma((per_dev, chunks, levels)), dma((cols, per_dev, chunks)),
            dma((chunks,)), dma((chunks,)),
            dma((members,)), dma((members,)),
        ],
        compiler_params=pltpu.CompilerParams(
            collective_id=0, has_side_effects=True, vmem_limit_bytes=60 * 1024 * 1024
        ),
        cost_estimate=pl.CostEstimate(
            flops=4 * tokens * tokens * depth + 2 * tokens * total * out_cols,
            bytes_accessed=2 * (3 * rows * total + total * out_cols + rows * members * out_cols),
            transcendentals=per_dev * tokens * tokens,
        ),
    )(head_class, kv_count, kv_blocks[0].transpose(1, 2, 0), queries[0], keys[0], values[0], weight)
    return result[None]


def solution(mesh):
    placed = (
        P("pipe", "seq", None),
        P("pipe", "seq", None),
        P("pipe", "seq", None),
        P("pipe", None, "seq"),
        P("pipe", None),
        P("pipe", None, None, None),
        P("pipe", None),
    )
    return jax.shard_map(
        functools.partial(shards, mesh.shape["pipe"]),
        mesh=mesh, in_specs=placed, out_specs=P("pipe", "seq", None), check_vma=False,
    )
```

profile of v0, /device:TPU:9, one launch (start us, length us, event | category | flops | bytes accessed | tf_op | source)
XLA Modules:
  0.0 110.8 jit_solution(3698962697298272922)
XLA Ops:
  0.0 108.8 %shard_map.73 = bf16[64,5120]{1,0:T(8,128)(2,1)} custom-call(s32[1,32]{1,0:T(1,128)} %classes.1, s32[1,32]{1,0:T(1,128)} %counts.1, s32[16,16,32]{2,1,0:T(8,128)} %bitcast.15, bf16[64,4096]{1,0:T(8,128)(2,1)} %bitcast.12, bf16[64,4096]{1,0:T(8,128)(2,1)} %bitcast.13, bf16[64,4096]{1,0:T(8,128)(2,1)} %bitcast.14, bf16[320,4096]{1,0:T(8,128)(2,1)} %bitcast.11), custom_call_target="tpu_custom_call" | custom-call | flops 3758096384 | bytes 4849664 | tf_op jit(solution)/shard_map/pallas_call | solution.py:388
  108.8 2.0 %copy.9 = bf16[1,64,5120]{2,1,0:T(8,128)(2,1)} copy(bf16[1,64,5120]{2,1,0:T(8,128)(2,1)} %bitcast.10) | data formatting | bytes 1310720
where the time goes:
time: 111 us
  Pallas kernels  109 us (98%)
  local copies, waits for them, and re-layouts  1.97 us (2%)
    pallas_call x1, Pallas kernels, shards(): pl.pallas_call(functools.partial(kernel, members, per_dev, stages), out_s...  109 us

commit v1 on v0

--- a/solution.py
+++ b/solution.py
@@ -195,8 +195,7 @@
             send_up(level, slot, chunk)
             send_down(level, slot, chunk)
             send_side(level, slot, chunk)
-            if then is not None:
-                then(chunk)
+            then(chunk)
             return carry
 
         lax.fori_loop(0, chunks, step, 0)
@@ -229,33 +228,38 @@
 
         lax.fori_loop(0, chunks, step, 0)
 
+    def swap_weight(column):
+        @pl.when(column < cols)
+        def _():
+            pltpu.make_async_remote_copy(
+                src_ref=weight.at[:, weight_columns(column, 1 - half)],
+                dst_ref=wboth.at[
+                    pl.ds(out_cols, out_cols),
+                    pl.ds(pl.multiple_of(column * depth, depth), depth),
+                ],
+                send_sem=w_sems.at[0],
+                recv_sem=w_sems.at[1],
+                device_id={"seq": partner},
+                device_id_type=MESH,
+            ).start()
+
     weight_span = wboth.at[pl.ds(out_cols, out_cols)]
     for slot in range(per_dev):
-        before = None
+        before = swap_weight
         if slot > 0:
             before = functools.partial(relay, slot - 1, first=1, last=2)
         attend(slot, before)
-        if slot == 0:
-
-            def swap_weight(column, carry):
-                pltpu.make_async_remote_copy(
-                    src_ref=weight.at[:, weight_columns(column, 1 - half)],
-                    dst_ref=wboth.at[
-                        pl.ds(out_cols, out_cols),
-                        pl.ds(pl.multiple_of(column * depth, depth), depth),
-                    ],
-                    send_sem=w_sems.at[0],
-                    recv_sem=w_sems.at[1],
-                    device_id={"seq": partner},
-                    device_id_type=MESH,
-                ).start()
-                return carry
-
-            lax.fori_loop(0, cols, swap_weight, 0)
-        else:
+        if slot > 0:
             relay_all(slot - 1, 2, levels - 1)
         if slot < per_dev - 1:
-            relay_all(slot, 0, 1)
+
+            def first_hop(chunk, carry):
+                relay(slot, chunk, 0, 1)
+                if slot == 0:
+                    swap_weight(chunks + chunk)
+                return carry
+
+            lax.fori_loop(0, chunks, first_hop, 0)
 
     def relay_last(chunk, carry):
         relay(per_dev - 1, chunk, 0, levels - 1)

time: 111 us -> 112 us (level)
  no operation moved by 1% of the time
where the time goes in v1:
time: 112 us; the launch traced here: 111 us
  Pallas kernels  109 us (97%)
  local copies, waits for them, and re-layouts  1.97 us (2%)
    pallas_call x1, Pallas kernels, shards(): pl.pallas_call(functools.partial(kernel, members, per_dev, stages), out_s...  109 us

profile of v1, /device:TPU:9, one launch (start us, length us, event | category | flops | bytes accessed | tf_op | source)
XLA Modules:
  0.0 111.3 jit_solution(10281925490349302126)
XLA Ops:
  0.0 109.4 %shard_map.73 = bf16[64,5120]{1,0:T(8,128)(2,1)} custom-call(s32[1,32]{1,0:T(1,128)} %classes.1, s32[1,32]{1,0:T(1,128)} %counts.1, s32[16,16,32]{2,1,0:T(8,128)} %bitcast.15, bf16[64,4096]{1,0:T(8,128)(2,1)} %bitcast.12, bf16[64,4096]{1,0:T(8,128)(2,1)} %bitcast.13, bf16[64,4096]{1,0:T(8,128)(2,1)} %bitcast.14, bf16[320,4096]{1,0:T(8,128)(2,1)} %bitcast.11), custom_call_target="tpu_custom_call" | custom-call | flops 3758096384 | bytes 4849664 | tf_op jit(solution)/shard_map/pallas_call | solution.py:392
  109.4 2.0 %copy.9 = bf16[1,64,5120]{2,1,0:T(8,128)(2,1)} copy(bf16[1,64,5120]{2,1,0:T(8,128)(2,1)} %bitcast.10) | data formatting | bytes 1310720

commit v2 on v1

--- a/solution.py
+++ b/solution.py
@@ -20,8 +20,8 @@
     members, per_dev, stages,
     classes, counts, lists, queries, keys, values, weight,
     out,
-    qbuf, kbuf, vbuf, ebuf, bbuf, abuf, wboth, cown, csend, crecv, osend, obuf,
-    qkv_send, qkv_recv, qkv_local, w_sems, w_local, up_send, down_send, side_send, a_recv,
+    staged, packed, heads_in, ebuf, bbuf, abuf, wboth, cown, csend, crecv, osend, obuf,
+    staging, qkv_send, qkv_recv, qkv_local, w_sems, w_local, up_send, down_send, side_send, a_recv,
     c_send, c_recv, o_send, o_recv,
 ):
     stage = lax.axis_index("pipe")
@@ -36,14 +36,20 @@
     across = me + 2 - 4 * side
     following = lax.rem(stage + 1, stages)
     preceding = lax.rem(stage + stages - 1, stages)
-    rows, width = queries.shape[0], kbuf.shape[-1]
+    rows, width = queries.shape[0], ebuf.shape[-1]
     tokens = rows * members
     depth = per_dev * width
     out_cols = weight.shape[0]
     tile = TILE
     chunks = tokens // tile
     group = tile // rows
-    tensors = ((queries, qbuf), (keys, kbuf), (values, vbuf))
+    tensors = (queries, keys, values)
+    loads = [
+        pltpu.make_async_copy(source, staged.at[which], staging.at[which])
+        for which, source in enumerate(tensors)
+    ]
+    for load in loads:
+        load.start()
 
     def block_at(chunk, place):
         return place * chunks + lax.rem(chunk + place, chunks)
@@ -63,37 +69,34 @@
     lax.fori_loop(1, members, greet, 0)
     lax.fori_loop(0, members, greet_preceding, 0)
 
-    def head_columns(owner, slot):
-        return pl.ds(pl.multiple_of((owner * per_dev + slot) * width, width), width)
-
     my_place = me // chunks
     my_chunk = lax.rem(lax.rem(me, chunks) + chunks * group - my_place, chunks)
-    mine = pl.ds(pl.multiple_of((my_chunk * group + my_place) * rows, rows), rows)
+    my_position = my_chunk * group + my_place
+    for which, load in enumerate(loads):
+        load.wait()
+        for head in range(per_dev * members):
+            packed[head, which] = staged[which, :, head * width : (head + 1) * width]
     own_copies = []
     for slot in range(per_dev):
-        for which, (source, landing) in enumerate(tensors):
-            copy = pltpu.make_async_copy(
-                source.at[:, head_columns(me, slot)],
-                landing.at[slot, mine],
-                qkv_local.at[slot, which],
-            )
-            copy.start()
-            own_copies.append(copy)
+        copy = pltpu.make_async_copy(
+            packed.at[me * per_dev + slot], heads_in.at[slot, my_position], qkv_local.at[slot]
+        )
+        copy.start()
+        own_copies.append(copy)
     pl.semaphore_wait(barrier, 2 * members - 1)
 
     for slot in range(per_dev):
 
         def send(r, carry):
             peer = lax.rem(me + r * (members // 2 - 1), members)
-            for which, (source, landing) in enumerate(tensors):
-                pltpu.make_async_remote_copy(
-                    src_ref=source.at[:, head_columns(peer, slot)],
-                    dst_ref=landing.at[slot, mine],
-                    send_sem=qkv_send.at[slot, which],
-                    recv_sem=qkv_recv.at[slot, which],
-                    device_id={"seq": peer},
-                    device_id_type=MESH,
-                ).start()
+            pltpu.make_async_remote_copy(
+                src_ref=packed.at[peer * per_dev + slot],
+                dst_ref=heads_in.at[slot, my_position],
+                send_sem=qkv_send.at[slot],
+                recv_sem=qkv_recv.at[slot],
+                device_id={"seq": peer},
+                device_id_type=MESH,
+            ).start()
             return carry
 
         lax.fori_loop(1, members, send, 0)
@@ -139,7 +142,7 @@
         copy.wait()
 
     scale = LOG2E * width ** (-0.5)
-    others = pl.ds(0, tokens - rows)
+    others = pl.ds(0, members - 1)
 
     def chunk_rows(chunk):
         return pl.ds(pl.multiple_of(chunk * tile, tile), tile)
@@ -174,21 +177,23 @@
         piece_copy(source_level, slot, chunk, across, side_send).start()
 
     def attend(slot, then):
-        for which, (source, landing) in enumerate(tensors):
-            span = landing.at[slot, others]
-            pltpu.make_async_copy(span, span, qkv_recv.at[slot, which]).wait()
+        span = heads_in.at[slot, others]
+        pltpu.make_async_copy(span, span, qkv_recv.at[slot]).wait()
 
         def step(chunk, carry):
             here = chunk_rows(chunk)
-            wide_query = jnp.concatenate([qbuf[slot, here], ebuf[slot, here]], axis=1)
-            wide_key = jnp.concatenate([kbuf[slot], bbuf[slot]], axis=1)
+            query = heads_in[slot, pl.ds(chunk * group, group), 0].reshape(tile, width)
+            key = heads_in[slot, :, 1].reshape(tokens, width)
+            value = heads_in[slot, :, 2].reshape(tokens, width)
+            wide_query = jnp.concatenate([query, ebuf[slot, here]], axis=1)
+            wide_key = jnp.concatenate([key, bbuf[slot]], axis=1)
             scores = lax.dot_general(
                 wide_query, wide_key, (((1,), (1,)), ((), ())), preferred_element_type=jnp.float32
             )
             top = jnp.max(scores, axis=1, keepdims=True)
             probs = jnp.exp2((scores - top) * scale).astype(jnp.bfloat16)
             wide_value = jnp.concatenate(
-                [vbuf[slot], jnp.ones((tokens, width), jnp.bfloat16)], axis=1
+                [value, jnp.ones((tokens, width), jnp.bfloat16)], axis=1
             )
             sums = jnp.dot(probs, wide_value, preferred_element_type=jnp.float32)
             abuf[col, slot, here] = (sums[:, :width] / sums[:, width:]).astype(jnp.bfloat16)
@@ -332,9 +337,8 @@
     hand(chunks - 1)
 
     for slot in range(per_dev):
-        for which, (source, landing) in enumerate(tensors):
-            span = landing.at[slot, others]
-            pltpu.make_async_copy(span, span, qkv_send.at[slot, which]).wait()
+        span = heads_in.at[slot, others]
+        pltpu.make_async_copy(span, span, qkv_send.at[slot]).wait()
     pltpu.make_async_copy(weight_span, weight_span, w_sems.at[0]).wait()
 
     def left(chunk, carry):
@@ -395,7 +399,10 @@
         in_specs=[smem, smem, vmem, hbm, hbm, hbm, hbm],
         out_specs=vmem,
         scratch_shapes=[
-            head_buffer, head_buffer, head_buffer, head_buffer, head_buffer,
+            pltpu.VMEM((3, rows, total), bf16),
+            pltpu.VMEM((heads, 3, rows, width), bf16),
+            pltpu.VMEM((per_dev, members, 3, rows, width), bf16),
+            head_buffer, head_buffer,
             pltpu.VMEM((cols, per_dev, tokens, width), bf16),
             pltpu.VMEM((2 * out_cols, cols * depth), bf16),
             pltpu.VMEM((tokens, out_cols), f32),
@@ -403,7 +410,7 @@
             pltpu.VMEM((tokens, out_cols), bf16),
             pltpu.VMEM((tokens, out_cols), bf16),
             pltpu.VMEM((members, rows, out_cols), bf16),
-            dma((per_dev, 3)), dma((per_dev, 3)), dma((per_dev, 3)),
+            dma((3,)), dma((per_dev,)), dma((per_dev,)), dma((per_dev,)),
             dma((2,)), dma,
             dma((per_dev, chunks, levels)), dma((per_dev, chunks, levels)),
             dma((per_dev, chunks, levels)), dma((cols, per_dev, chunks)),

time: 112 us -> 111 us (level)
  no operation moved by 1% of the time
where the time goes in v2:
time: 111 us
  Pallas kernels  109 us (98%)
  local copies, waits for them, and re-layouts  1.97 us (2%)
    pallas_call x1, Pallas kernels, shards(): pl.pallas_call(functools.partial(kernel, members, per_dev, stages), out_s...  109 us

profile of v2, /device:TPU:9, one launch (start us, length us, event | category | flops | bytes accessed | tf_op | source)
XLA Modules:
  0.0 111.0 jit_solution(17580718150362806861)
XLA Ops:
  0.0 109.1 %shard_map.73 = bf16[64,5120]{1,0:T(8,128)(2,1)} custom-call(s32[1,32]{1,0:T(1,128)} %classes.1, s32[1,32]{1,0:T(1,128)} %counts.1, s32[16,16,32]{2,1,0:T(8,128)} %bitcast.15, bf16[64,4096]{1,0:T(8,128)(2,1)} %bitcast.12, bf16[64,4096]{1,0:T(8,128)(2,1)} %bitcast.13, bf16[64,4096]{1,0:T(8,128)(2,1)} %bitcast.14, bf16[320,4096]{1,0:T(8,128)(2,1)} %bitcast.11), custom_call_target="tpu_custom_call" | custom-call | flops 3758096384 | bytes 4849664 | tf_op jit(solution)/shard_map/pallas_call | solution.py:396
  109.1 2.0 %copy.9 = bf16[1,64,5120]{2,1,0:T(8,128)(2,1)} copy(bf16[1,64,5120]{2,1,0:T(8,128)(2,1)} %bitcast.10) | data formatting | bytes 1310720

commit v3 on v2

--- a/solution.py
+++ b/solution.py
@@ -26,14 +26,17 @@
 ):
     stage = lax.axis_index("pipe")
     me = lax.axis_index("seq")
-    half = lax.rem(me, 2)
-    col = me // 2
-    side = lax.rem(col, 2)
-    level = col // 2
+    odd = lax.rem(stage, 2)
+    half_step, side_step = 1 + odd, 2 - odd
+    bits = (lax.rem(me, 2), lax.rem(me // 2, 2))
+    half = bits[0] + odd * (bits[1] - bits[0])
+    side = bits[1] + odd * (bits[0] - bits[1])
+    level = me // 4
     levels = members // 4
     cols = members // 2
-    partner = me + 1 - 2 * half
-    across = me + 2 - 4 * side
+    col = 2 * level + side
+    partner = me + half_step * (1 - 2 * half)
+    across = me + side_step * (1 - 2 * side)
     following = lax.rem(stage + 1, stages)
     preceding = lax.rem(stage + stages - 1, stages)
     rows, width = queries.shape[0], ebuf.shape[-1]
@@ -85,6 +88,24 @@
         own_copies.append(copy)
     pl.semaphore_wait(barrier, 2 * members - 1)
 
+    def weight_columns(column, which_half):
+        owner = (column // 2) * 4 + lax.rem(column, 2) * side_step + which_half * half_step
+        return pl.ds(pl.multiple_of(owner * depth, depth), depth)
+
+    def swap_weight(column, carry):
+        pltpu.make_async_remote_copy(
+            src_ref=weight.at[:, weight_columns(column, 1 - half)],
+            dst_ref=wboth.at[
+                pl.ds(out_cols, out_cols),
+                pl.ds(pl.multiple_of(column * depth, depth), depth),
+            ],
+            send_sem=w_sems.at[0],
+            recv_sem=w_sems.at[1],
+            device_id={"seq": partner},
+            device_id_type=MESH,
+        ).start()
+        return carry
+
     for slot in range(per_dev):
 
         def send(r, carry):
@@ -100,9 +121,8 @@
             return carry
 
         lax.fori_loop(1, members, send, 0)
-
-    def weight_columns(column, which_half):
-        return pl.ds(pl.multiple_of((2 * column + which_half) * depth, depth), depth)
+        if slot == 0:
+            lax.fori_loop(0, cols, swap_weight, 0)
 
     def own_weight(column, carry):
         pltpu.make_async_copy(
@@ -200,7 +220,8 @@
             send_up(level, slot, chunk)
             send_down(level, slot, chunk)
             send_side(level, slot, chunk)
-            then(chunk)
+            if then is not None:
+                then(chunk)
             return carry
 
         lax.fori_loop(0, chunks, step, 0)
@@ -233,38 +254,16 @@
 
         lax.fori_loop(0, chunks, step, 0)
 
-    def swap_weight(column):
-        @pl.when(column < cols)
-        def _():
-            pltpu.make_async_remote_copy(
-                src_ref=weight.at[:, weight_columns(column, 1 - half)],
-                dst_ref=wboth.at[
-                    pl.ds(out_cols, out_cols),
-                    pl.ds(pl.multiple_of(column * depth, depth), depth),
-                ],
-                send_sem=w_sems.at[0],
-                recv_sem=w_sems.at[1],
-                device_id={"seq": partner},
-                device_id_type=MESH,
-            ).start()
-
     weight_span = wboth.at[pl.ds(out_cols, out_cols)]
     for slot in range(per_dev):
-        before = swap_weight
+        before = None
         if slot > 0:
             before = functools.partial(relay, slot - 1, first=1, last=2)
         attend(slot, before)
         if slot > 0:
             relay_all(slot - 1, 2, levels - 1)
         if slot < per_dev - 1:
-
-            def first_hop(chunk, carry):
-                relay(slot, chunk, 0, 1)
-                if slot == 0:
-                    swap_weight(chunks + chunk)
-                return carry
-
-            lax.fori_loop(0, chunks, first_hop, 0)
+            relay_all(slot, 0, 1)
 
     def relay_last(chunk, carry):
         relay(per_dev - 1, chunk, 0, levels - 1)

time: 111 us -> 105 us (0.946); the launches traced: 111 us -> 103 us
  Pallas kernels: 109 us -> 101 us
    pallas_call x1, Pallas kernels: 109 us -> 101 us  [shards(): pl.pallas_call(functools.partial(kernel, members, per_dev, stages), out_s...]
where the time goes in v3:
time: 105 us; the launch traced here: 103 us
  Pallas kernels  101 us (96%)
  local copies, waits for them, and re-layouts  1.97 us (2%)
    pallas_call x1, Pallas kernels, shards(): pl.pallas_call(functools.partial(kernel, members, per_dev, stages), out_s...  101 us

profile of v3, /device:TPU:9, one launch (start us, length us, event | category | flops | bytes accessed | tf_op | source)
XLA Modules:
  0.0 103.2 jit_solution(6852769654941667330)
XLA Ops:
  0.0 101.2 %shard_map.73 = bf16[64,5120]{1,0:T(8,128)(2,1)} custom-call(s32[1,32]{1,0:T(1,128)} %classes.1, s32[1,32]{1,0:T(1,128)} %counts.1, s32[16,16,32]{2,1,0:T(8,128)} %bitcast.15, bf16[64,4096]{1,0:T(8,128)(2,1)} %bitcast.12, bf16[64,4096]{1,0:T(8,128)(2,1)} %bitcast.13, bf16[64,4096]{1,0:T(8,128)(2,1)} %bitcast.14, bf16[320,4096]{1,0:T(8,128)(2,1)} %bitcast.11), custom_call_target="tpu_custom_call" | custom-call | flops 3758096384 | bytes 4849664 | tf_op jit(solution)/shard_map/pallas_call | solution.py:395
  101.2 2.0 %copy.9 = bf16[1,64,5120]{2,1,0:T(8,128)(2,1)} copy(bf16[1,64,5120]{2,1,0:T(8,128)(2,1)} %bitcast.10) | data formatting | bytes 1310720

commit v4 on v3

--- a/solution.py
+++ b/solution.py
@@ -12,7 +12,6 @@
 MASKED = 131072.0
 LOG2E = 1.4426950408889634
 TILE = 256
-AHEAD = 3
 MESH = pl.DeviceIdType.MESH
 
 
@@ -20,7 +19,7 @@
     members, per_dev, stages,
     classes, counts, lists, queries, keys, values, weight,
     out,
-    staged, packed, heads_in, ebuf, bbuf, abuf, wboth, cown, csend, crecv, osend, obuf,
+    staged, packed, heads_in, ebuf, bbuf, abuf, wboth, cacc, cown, csend, crecv, osend, obuf,
     staging, qkv_send, qkv_recv, qkv_local, w_sems, w_local, up_send, down_send, side_send, a_recv,
     c_send, c_recv, o_send, o_recv,
 ):
@@ -265,11 +264,6 @@
         if slot < per_dev - 1:
             relay_all(slot, 0, 1)
 
-    def relay_last(chunk, carry):
-        relay(per_dev - 1, chunk, 0, levels - 1)
-        return carry
-
-    lax.fori_loop(0, AHEAD, relay_last, 0)
     weight_own = wboth.at[pl.ds(0, out_cols)]
     pltpu.make_async_copy(weight_own, weight_own, w_local).wait()
     pltpu.make_async_copy(weight_span, weight_span, w_sems.at[1]).wait()
@@ -303,25 +297,31 @@
         for q in range(group):
             row_copy(chunk, lax.rem(level + q, group)).start()
 
+    def share(slot, chunk):
+        def from_side(source_level, inner):
+            received(2 * source_level + 1 - side, slot, chunk)
+            return inner
+
+        lax.fori_loop(0, levels, from_side, 0)
+        here = chunk_rows(chunk)
+        piece = jnp.concatenate([abuf[column, slot, here] for column in range(cols)], axis=1)
+        starts = [column * depth + slot * width for column in range(cols)]
+        columns = jnp.concatenate([wboth[:, start : start + width] for start in starts], axis=1)
+        return lax.dot_general(
+            piece, columns, (((1,), (1,)), ((), ())), preferred_element_type=jnp.float32
+        )
+
+    def prepare(chunk, carry):
+        relay(per_dev - 1, chunk, 0, levels - 1)
+        total = share(0, chunk)
+        for slot in range(1, per_dev - 1):
+            total += share(slot, chunk)
+        cacc[chunk_rows(chunk)] = total
+        return carry
+
     def finish(chunk, carry):
         here = chunk_rows(chunk)
-
-        @pl.when(chunk + AHEAD < chunks)
-        def _():
-            relay_last(chunk + AHEAD, 0)
-
-        def from_side(source_level, inner):
-            for slot in range(per_dev):
-                received(2 * source_level + 1 - side, slot, chunk)
-            return inner
-
-        lax.fori_loop(0, levels, from_side, 0)
-        piece = jnp.concatenate(
-            [abuf[column, slot, here] for column in range(cols) for slot in range(per_dev)], axis=1
-        )
-        shares = lax.dot_general(
-            piece, wboth[...], (((1,), (1,)), ((), ())), preferred_element_type=jnp.float32
-        )
+        shares = cacc[here] + share(per_dev - 1, chunk)
         csend[here] = shares[:, out_cols:].astype(jnp.bfloat16)
         chunk_copy(chunk).start()
         cown[here] = shares[:, :out_cols]
@@ -332,6 +332,7 @@
 
         return carry
 
+    lax.fori_loop(0, chunks, prepare, 0)
     lax.fori_loop(0, chunks, finish, 0)
     hand(chunks - 1)
 
@@ -388,7 +389,7 @@
     dma = pltpu.SemaphoreType.DMA
     vmem = pl.BlockSpec(memory_space=pltpu.VMEM)
     smem = pl.BlockSpec(memory_space=pltpu.SMEM)
-    hbm = pl.BlockSpec(memory_space=pl.ANY)
+    hbm = pl.BlockSpec(memory_space=pltpu.HBM)
     head_buffer = pltpu.VMEM((per_dev, tokens, width), bf16)
     levels = members // 4
     chunks = tokens // TILE
@@ -404,6 +405,7 @@
             head_buffer, head_buffer,
             pltpu.VMEM((cols, per_dev, tokens, width), bf16),
             pltpu.VMEM((2 * out_cols, cols * depth), bf16),
+            pltpu.VMEM((tokens, 2 * out_cols), f32),
             pltpu.VMEM((tokens, out_cols), f32),
             pltpu.VMEM((tokens, out_cols), bf16),
             pltpu.VMEM((tokens, out_cols), bf16),
@@ -417,7 +419,7 @@
             dma((members,)), dma((members,)),
         ],
         compiler_params=pltpu.CompilerParams(
-            collective_id=0, has_side_effects=True, vmem_limit_bytes=60 * 1024 * 1024
+            collective_id=0, has_side_effects=True, vmem_limit_bytes=48 * 1024 * 1024
         ),
         cost_estimate=pl.CostEstimate(
             flops=4 * tokens * tokens * depth + 2 * tokens * total * out_cols,

time: 105 us -> 110 us (1.048); the launches traced: 103 us -> 110 us
  local copies, waits for them, and re-layouts: 1.97 us -> 7.91 us
    unnamed x1 -> x15, local copies, waits for them, and re-layouts: 1.97 us -> 7.91 us
where the time goes in v4:
time: 110 us
  Pallas kernels  102 us (93%)
  local copies, waits for them, and re-layouts  7.91 us (7%)
    pallas_call x1, Pallas kernels, shards(): pl.pallas_call(functools.partial(kernel, members, per_dev, stages), out_s...  102 us
    unnamed x15, local copies, waits for them, and re-layouts  7.91 us

profile of v4, /device:TPU:9, one launch (start us, length us, event | category | flops | bytes accessed | tf_op | source)
XLA Modules:
  0.0 110.0 jit_solution(14941828328664995532)
XLA Ops:
  0.0 0.0 copy-start
  0.0 1.7 %copy-done = bf16[1,4096,320]{1,2,0:T(8,128)(2,1)S(1)} copy-done((bf16[1,4096,320]{1,2,0:T(8,128)(2,1)S(1)}, bf16[1,4096,320]{1,2,0:T(8,128)(2,1)}, u32[]{:S(2)}) %copy-start) | copy-done | bytes 2621464
  1.7 0.0 copy-start.1
  1.7 1.0 copy-done.1
  2.8 0.0 copy-start.2
  2.8 1.0 copy-done.2
  3.8 0.0 copy-start.3
  3.8 1.0 copy-done.3
  4.9 0.0 copy-start.4
  4.9 0.9 copy-done.4
  5.8 0.0 copy-start.5
  5.8 0.7 copy-done.5
  6.4 0.0 copy-start.6
  6.4 0.7 copy-done.6
  7.1 102.1 %shard_map.73 = bf16[64,5120]{1,0:T(8,128)(2,1)S(1)} custom-call(s32[1,32]{1,0:T(1,128)S(1)} %copy-done.5, s32[1,32]{1,0:T(1,128)S(1)} %copy-done.6, s32[16,16,32]{2,1,0:T(8,128)S(1)} %bitcast.15, bf16[64,4096]{1,0:T(8,128)(2,1)S(1)} %bitcast.12, bf16[64,4096]{1,0:T(8,128)(2,1)S(1)} %bitcast.13, bf16[64,4096]{1,0:T(8,128)(2,1)S(1)} %bitcast.14, ...), custom_call_target="tpu_custom_call" | custom-call | flops 3758096384 | bytes 4849664 | tf_op jit(solution)/shard_map/pallas_call | solution.py:396
  109.2 0.8 copy.9
Async XLA Ops:
  0.0 1.7 %copy-start = (bf16[1,4096,320]{1,2,0:T(8,128)(2,1)S(1)}, bf16[1,4096,320]{1,2,0:T(8,128)(2,1)}, u32[]{:S(2)}) copy-start(bf16[1,4096,320]{1,2,0:T(8,128)(2,1)} %param.10) | copy-start | bytes 7864324
  1.7 1.0 copy-start.1
  2.8 1.0 copy-start.2
  3.8 1.0 copy-start.3
  4.9 0.9 copy-start.4
  5.8 0.7 copy-start.5
  6.4 0.7 copy-start.6

commit v5 on v3

--- a/solution.py
+++ b/solution.py
@@ -12,7 +12,6 @@
 MASKED = 131072.0
 LOG2E = 1.4426950408889634
 TILE = 256
-AHEAD = 3
 MESH = pl.DeviceIdType.MESH
 
 
@@ -247,29 +246,30 @@
 
         lax.fori_loop(first, last, hop, 0)
 
-    def relay_all(slot, first, last):
-        def step(chunk, carry):
-            relay(slot, chunk, first, last)
+    def wave(n):
+        def hop(t, carry):
+            piece = n - 1 - t
+
+            @pl.when((piece >= 0) & (piece < per_dev * chunks))
+            def _():
+                relay(piece // chunks, lax.rem(piece, chunks), t, t + 1)
+
             return carry
 
-        lax.fori_loop(0, chunks, step, 0)
+        lax.fori_loop(0, levels - 1, hop, 0)
 
     weight_span = wboth.at[pl.ds(out_cols, out_cols)]
     for slot in range(per_dev):
-        before = None
         if slot > 0:
-            before = functools.partial(relay, slot - 1, first=1, last=2)
-        attend(slot, before)
-        if slot > 0:
-            relay_all(slot - 1, 2, levels - 1)
-        if slot < per_dev - 1:
-            relay_all(slot, 0, 1)
-
-    def relay_last(chunk, carry):
-        relay(per_dev - 1, chunk, 0, levels - 1)
-        return carry
-
-    lax.fori_loop(0, AHEAD, relay_last, 0)
+            wave(slot * chunks)
+
+        def after(chunk, slot=slot):
+            @pl.when(chunk > 0)
+            def _():
+                wave(slot * chunks + chunk)
+
+        attend(slot, after)
+
     weight_own = wboth.at[pl.ds(0, out_cols)]
     pltpu.make_async_copy(weight_own, weight_own, w_local).wait()
     pltpu.make_async_copy(weight_span, weight_span, w_sems.at[1]).wait()
@@ -306,9 +306,7 @@
     def finish(chunk, carry):
         here = chunk_rows(chunk)
 
-        @pl.when(chunk + AHEAD < chunks)
-        def _():
-            relay_last(chunk + AHEAD, 0)
+        wave(per_dev * chunks + chunk)
 
         def from_side(source_level, inner):
             for slot in range(per_dev):

time: 105 us -> 107 us (1.019)
  Pallas kernels: 101 us -> 104 us
    pallas_call x1, Pallas kernels: 101 us -> 104 us  [shards(): pl.pallas_call(functools.partial(kernel, members, per_dev, stages), out_s...]
where the time goes in v5:
time: 107 us; the launch traced here: 106 us
  Pallas kernels  104 us (97%)
  local copies, waits for them, and re-layouts  1.97 us (2%)
    pallas_call x1, Pallas kernels, shards(): pl.pallas_call(functools.partial(kernel, members, per_dev, stages), out_s...  104 us

profile of v5, /device:TPU:9, one launch (start us, length us, event | category | flops | bytes accessed | tf_op | source)
XLA Modules:
  0.0 106.1 jit_solution(6895712164297996151)
XLA Ops:
  0.0 104.1 %shard_map.73 = bf16[64,5120]{1,0:T(8,128)(2,1)} custom-call(s32[1,32]{1,0:T(1,128)} %classes.1, s32[1,32]{1,0:T(1,128)} %counts.1, s32[16,16,32]{2,1,0:T(8,128)} %bitcast.15, bf16[64,4096]{1,0:T(8,128)(2,1)} %bitcast.12, bf16[64,4096]{1,0:T(8,128)(2,1)} %bitcast.13, bf16[64,4096]{1,0:T(8,128)(2,1)} %bitcast.14, bf16[320,4096]{1,0:T(8,128)(2,1)} %bitcast.11), custom_call_target="tpu_custom_call" | custom-call | flops 3758096384 | bytes 4849664 | tf_op jit(solution)/shard_map/pallas_call | solution.py:393
  104.1 2.0 %copy.9 = bf16[1,64,5120]{2,1,0:T(8,128)(2,1)} copy(bf16[1,64,5120]{2,1,0:T(8,128)(2,1)} %bitcast.10) | data formatting | bytes 1310720

commit v6 on v3

--- a/solution.py
+++ b/solution.py
@@ -12,7 +12,6 @@
 MASKED = 131072.0
 LOG2E = 1.4426950408889634
 TILE = 256
-AHEAD = 3
 MESH = pl.DeviceIdType.MESH
 
 
@@ -265,11 +264,17 @@
         if slot < per_dev - 1:
             relay_all(slot, 0, 1)
 
-    def relay_last(chunk, carry):
-        relay(per_dev - 1, chunk, 0, levels - 1)
-        return carry
-
-    lax.fori_loop(0, AHEAD, relay_last, 0)
+    def wave(n, carry):
+        def hop(t, inner):
+            @pl.when((n >= t) & (n - t < chunks))
+            def _():
+                relay(per_dev - 1, n - t, t, t + 1)
+
+            return inner
+
+        return lax.fori_loop(0, levels - 1, hop, carry)
+
+    lax.fori_loop(0, levels - 1, wave, 0)
     weight_own = wboth.at[pl.ds(0, out_cols)]
     pltpu.make_async_copy(weight_own, weight_own, w_local).wait()
     pltpu.make_async_copy(weight_span, weight_span, w_sems.at[1]).wait()
@@ -306,9 +311,7 @@
     def finish(chunk, carry):
         here = chunk_rows(chunk)
 
-        @pl.when(chunk + AHEAD < chunks)
-        def _():
-            relay_last(chunk + AHEAD, 0)
+        wave(chunk + levels - 1, 0)
 
         def from_side(source_level, inner):
             for slot in range(per_dev):

time: 105 us -> 103 us (0.981); the launches traced: 103 us -> 103 us
  no operation moved by 1% of the time
where the time goes in v6:
time: 103 us
  Pallas kernels  101 us (98%)
  local copies, waits for them, and re-layouts  1.97 us (2%)
    pallas_call x1, Pallas kernels, shards(): pl.pallas_call(functools.partial(kernel, members, per_dev, stages), out_s...  101 us

profile of v6, /device:TPU:9, one launch (start us, length us, event | category | flops | bytes accessed | tf_op | source)
XLA Modules:
  0.0 103.0 jit_solution(13449675195842096251)
XLA Ops:
  0.0 101.0 %shard_map.73 = bf16[64,5120]{1,0:T(8,128)(2,1)} custom-call(s32[1,32]{1,0:T(1,128)} %classes.1, s32[1,32]{1,0:T(1,128)} %counts.1, s32[16,16,32]{2,1,0:T(8,128)} %bitcast.15, bf16[64,4096]{1,0:T(8,128)(2,1)} %bitcast.12, bf16[64,4096]{1,0:T(8,128)(2,1)} %bitcast.13, bf16[64,4096]{1,0:T(8,128)(2,1)} %bitcast.14, bf16[320,4096]{1,0:T(8,128)(2,1)} %bitcast.11), custom_call_target="tpu_custom_call" | custom-call | flops 3758096384 | bytes 4849664 | tf_op jit(solution)/shard_map/pallas_call | solution.py:398
  101.0 2.0 %copy.9 = bf16[1,64,5120]{2,1,0:T(8,128)(2,1)} copy(bf16[1,64,5120]{2,1,0:T(8,128)(2,1)} %bitcast.10) | data formatting | bytes 1310720
